TPU v7x, 512 devices: a whole 4x4x16 slice. The times are simulated.
512 devices in a mesh: pix: 16 (over y, x_lo, core), frame: 32 (over x_hi, z).
Axes of the slice: x: 4 (x_hi: 2, x_lo: 2; x = x_hi * 2 + x_lo), y: 4, z: 16, core: 2. Of those that a mesh axis runs over, the one named last changes fastest.
Arguments:
- frames: float32 [2048, 20480], P('frame', 'pix')
- start_basis: float32 [2048, 128], P('frame'), may hold values from -0.125 to 0.125
- picks: int32 [128], replicated, may hold values from 0 to 2047, as said below
- conv_in: bfloat16 [64, 9], replicated, may hold values from -2 to 2
- bias_in: float32 [64], replicated, may hold values from -3 to 3
- conv_out: bfloat16 [9, 64], replicated, may hold values from -0.25 to 0.25
- bias_out: float32 [1], replicated, may hold values from -1 to 1
Outputs:
- coeffs: float32 [2048, 128], P('frame')
- scores: float32 [128, 20480], P('frame', 'pix')
Inputs may be any that keep to these rules, and one draw needn't show every extreme that they name: `picks`: indices may repeat; 0 and 2047 occur in every draw.
All inputs are finite; a program needn't handle non-finite values.
Results may differ from a plain program's by a relative error of at most 0.0013.
Values may be sent and summed in bfloat16 or wider, within the bound.
A program may use at most 64 MiB of HBM per device.

v0:
```python
import jax
import jax.numpy as jnp
from jax import lax
from jax.sharding import PartitionSpec as P

W = 640
HID = 64
ITERS = 2


threshold = 0.5


def extended_2(x, sides, width):
    for axis, dim in sides:
        count, length = (lax.axis_size(axis), x.shape[dim])
        up = [(i, (i + 1) % count) for i in range(count - 1)]
        down = [(j, i) for i, j in up]
        last = lax.slice_in_dim(x, length - width, length, axis=dim)
        leading = lax.slice_in_dim(x, 0, width, axis=dim)
        before = lax.ppermute(last, axis, up)
        after = lax.ppermute(leading, axis, down)
        x = jnp.concatenate([before, x, after], axis=dim)
    return x


def inner(left, right):
    return lax.dot_general(
        left,
        right,
        (((0,), (0,)), ((), ())),
        precision=lax.Precision.HIGHEST,
        preferred_element_type=jnp.float32,
    )


def product(left, right):
    return jnp.dot(left, right, precision=lax.Precision.HIGHEST, preferred_element_type=jnp.float32)


def outer_rows(left, right):
    return lax.dot_general(
        left,
        right,
        (((1,), (1,)), ((), ())),
        precision=lax.Precision.HIGHEST,
        preferred_element_type=jnp.float32,
    )


def solve_factor(factor, block):
    return lax.linalg.triangular_solve(factor, block, left_side=False, lower=True, transpose_a=True)


def orthonormal(block, gram):
    return solve_factor(jnp.linalg.cholesky(gram), block)


def shrink(values):
    return (jnp.sign(values) * jnp.maximum(jnp.abs(values) - threshold, 0.0)).astype(jnp.bfloat16)


def pick_rows(shrunk, wanted_ids, row_count):
    columns = lax.broadcasted_iota(jnp.int32, (row_count, shrunk.shape[0]), 1)
    onehot = (wanted_ids[:, None] == columns).astype(jnp.bfloat16)
    return jnp.dot(onehot, shrunk, preferred_element_type=jnp.float32)


def first_layer(image, conv_in, bias_in):
    rows_out = image.shape[0] - 2
    padded = jnp.pad(image, ((0, 0), (1, 1)))
    stacked = jnp.stack(
        [
            padded[row_shift : row_shift + rows_out, col_shift : col_shift + W]
            for row_shift in range(3)
            for col_shift in range(3)
        ]
    )
    summed = (
        jnp.dot(conv_in, stacked.reshape(9, rows_out * W), preferred_element_type=jnp.float32)
        + bias_in[:, None]
    )
    return jnp.maximum(summed, 0.0).astype(jnp.bfloat16).reshape(HID, rows_out, W)


def second_layer(hidden, conv_out, bias_out):
    rows_in = hidden.shape[1]
    rows_out = rows_in - 2
    tapped = jnp.dot(
        conv_out, hidden.reshape(HID, rows_in * W), preferred_element_type=jnp.float32
    ).reshape(9, rows_in, W)
    padded = jnp.pad(tapped, ((0, 0), (0, 0), (1, 1)))
    total = jnp.zeros((rows_out, W), jnp.float32)
    for row_shift in range(3):
        for col_shift in range(3):
            total = (
                total
                + padded[
                    row_shift * 3 + col_shift,
                    row_shift : row_shift + rows_out,
                    col_shift : col_shift + W,
                ]
            )
    return (total + bias_out[0]).reshape(-1)


def shards(frames, start_basis, picks, conv_in, bias_in, conv_out, bias_out):
    local_frames, local_pixels = frames.shape
    frame_groups = lax.axis_size("frame")
    group_index = lax.axis_index("frame")
    sel_local = picks.shape[0] // frame_groups
    local_rows = local_pixels // W
    coeffs = None
    ortho = None
    omega = start_basis
    for step in range(ITERS):
        if step > 0:
            omega = coeffs
        basis = lax.psum(inner(frames, omega), "frame")
        ortho = orthonormal(basis, lax.psum(inner(basis, basis), "pix"))
        coeffs = lax.psum(product(frames, ortho), "pix")
    residual = frames - outer_rows(coeffs, ortho)
    wanted_ids = picks - group_index * local_frames
    routed = lax.psum_scatter(
        pick_rows(shrink(residual), wanted_ids, sel_local * lax.axis_size("frame")).astype(
            jnp.bfloat16
        ),
        "frame",
        scatter_dimension=0,
        tiled=True,
    )
    images = routed.reshape(sel_local, local_rows, W)
    extended = extended_2(images, (("pix", 1),), 1)

    def score_one(image):
        hidden = first_layer(image, conv_in, bias_in)
        hidden = extended_2(hidden, (("pix", 1),), 1)
        return second_layer(hidden, conv_out, bias_out)

    scores = lax.map(score_one, extended)
    return (coeffs, scores)


def solution(mesh):
    placed = (P("frame", "pix"), P("frame", None), P(), P(), P(), P(), P())
    return jax.shard_map(
        shards,
        mesh=mesh,
        in_specs=placed,
        out_specs=(P("frame", None), P("frame", "pix")),
        check_vma=False,
    )
```

profile of v0, /device:TPU:1, one launch (start us, length us, event | category | flops | bytes accessed | tf_op | source)
XLA Modules:
  0.0 1338.5 jit_solution(7017913151556980267)
XLA Ops:
  7.9 3.0 fusion.22
  11.0 278.5 %all-reduce.9.cloned.1.call-done = f32[1280,128]{1,0:T(8,128)} async-done(((f32[1280,128]{1,0:T(8,128)}), f32[1280,128]{1,0:T(8,128)}) %all-reduce.9.cloned.1.call-update) | async-done | bytes 655376 | tf_op jit(solution)/shard_map/psum | solution.py:119
  289.5 3.2 fusion.23
  292.8 134.3 %all-reduce.11.cloned.1.call-done = f32[128,128]{0,1:T(8,128)} async-done(((f32[128,128]{0,1:T(8,128)}), f32[128,128]{0,1:T(8,128)}) %all-reduce.11.cloned.1.call-update) | async-done | bytes 65552 | tf_op jit(solution)/shard_map/psum | solution.py:120
  428.1 11.7 cholesky.44
  441.2 9.8 custom-call.6
  452.6 51.4 %psum.44 = f32[64,128]{0,1:T(8,128)S(1)} all-reduce(f32[64,128]{0,1:T(8,128)S(1)} %convolution_bitcast_fusion.4), channel_id=1, replica_groups=mesh['pix'=16,'frame'=32] {'pix'}, use_global_device_ids=true, to_apply=%region_4.7 | all-reduce | flops 8192 | bytes 65536 | tf_op jit(solution)/shard_map/psum | solution.py:121
  505.6 274.8 %all-reduce.13.cloned.1.call-done = f32[1280,128]{0,1:T(8,128)} async-done(((f32[1280,128]{0,1:T(8,128)}), f32[1280,128]{0,1:T(8,128)}) %all-reduce.13.cloned.1.call-update) | async-done | bytes 655376 | tf_op jit(solution)/shard_map/psum | solution.py:119
  780.4 2.7 fusion.24
  783.7 133.9 %all-reduce.15.cloned.1.call-done = f32[128,128]{0,1:T(8,128)} async-done(((f32[128,128]{0,1:T(8,128)}), f32[128,128]{0,1:T(8,128)}) %all-reduce.15.cloned.1.call-update) | async-done | bytes 65552 | tf_op jit(solution)/shard_map/psum | solution.py:120
  918.7 11.7 cholesky.55
  931.8 9.8 custom-call.7
  943.1 51.3 %psum.47 = f32[64,128]{1,0:T(8,128)S(1)} all-reduce(f32[64,128]{1,0:T(8,128)S(1)} %convolution_bitcast_fusion.5), channel_id=1, replica_groups=mesh['pix'=16,'frame'=32] {'pix'}, use_global_device_ids=true, to_apply=%region_7.10 | all-reduce | flops 8192 | bytes 65536 | tf_op jit(solution)/shard_map/psum | solution.py:121
  998.0 262.0 %all-reduce.17.cloned.1.call-done = bf16[128,1280]{1,0:T(8,128)(2,1)} async-done(((bf16[128,1280]{1,0:T(8,128)(2,1)}), bf16[128,1280]{1,0:T(8,128)(2,1)}) %all-reduce.17.cloned.1.call-update) | async-done | bytes 327696
  1260.7 21.7 %collective-permute-start.2 = (bf16[4,1,640]{2,1,0:T(2,128)(2,1)S(1)}, bf16[4,1,640]{2,1,0:T(2,128)(2,1)S(1)}, u32[]{:S(2)}, u32[]{:S(2)}) collective-permute-start(bf16[4,1,640]{2,1,0:T(2,128)(2,1)S(1)} %get-tuple-element.120), channel_id=1, source_target_pairs={{0,32},{32,64},{64,96},{96,128},{128,160},{160,192},{192,224},{224... | collective-permute-start | bytes 15368 | tf_op jit(solution)/shard_map/ppermute | solution.py:21
  1282.4 1.9 collective-permute-start.3
  1284.4 3.0 collective-permute-done.3
  1287.5 43.9 %while.12 = (s32[]{:T(128)}, f32[4,1280]{1,0:T(4,128)S(1)}, bf16[4,4,640]{2,1,0:T(4,128)(2,1)S(1)}, bf16[64,9]{0,1:T(8,128)(2,1)S(1)}, f32[64]{0:T(128)S(1)}, /*...) while((s32[]{:T(128)}, f32[4,1280]{1,0:T(4,128)S(1)}, ...), condition=%wide.region_10.13_spmd, body=%wide.region_9.12_spmd.sunk | while | flops 5664004 | bytes 3686645 | solution.py:140
  1288.4 1.9 collective-permute-start
  1290.3 3.6 collective-permute-start.1
  1298.8 1.9 collective-permute-start
  1300.7 4.4 collective-permute-start.1
  1311.9 4.4 collective-permute-start.1
  1323.1 4.4 collective-permute-start.1
  (161 shorter events, 37.7 us)
Async XLA Ops:
  7.2 0.8 copy-start
  7.2 282.3 %all-reduce.9.cloned.1.call-start = ((), (), s32[]{:S(2)}) async-start(), calls=%async_computation | async-start | bytes 1310720 | tf_op jit(solution)/shard_map/psum | solution.py:119
  11.0 416.1 %all-reduce.11.cloned.1.call-start = ((), (), s32[]{:S(2)}) async-start(), calls=%async_computation.1 | async-start | bytes 131072 | tf_op jit(solution)/shard_map/psum | solution.py:120
  289.5 161.5 %copy-start.3 = (f32[1280,128]{1,0:T(8,128)S(1)}, f32[1280,128]{1,0:T(8,128)}, u32[]{:S(2)}) copy-start(f32[1280,128]{1,0:T(8,128)} %all-reduce.9.cloned.1.call-done) | copy-start | bytes 1966084
  292.7 487.7 %all-reduce.13.cloned.1.call-start = ((), (), s32[]{:S(2)}) async-start(), calls=%async_computation.2 | async-start | bytes 1310720 | tf_op jit(solution)/shard_map/psum | solution.py:119
  427.1 1.0 copy-start.5
  451.0 1.0 copy-start.1
  505.5 412.1 %all-reduce.15.cloned.1.call-start = ((), (), s32[]{:S(2)}) async-start(), calls=%async_computation.3 | async-start | bytes 131072 | tf_op jit(solution)/shard_map/psum | solution.py:120
  780.4 161.2 %copy-start.2 = (f32[1280,128]{0,1:T(8,128)S(1)}, f32[1280,128]{0,1:T(8,128)}, u32[]{:S(2)}) copy-start(f32[1280,128]{0,1:T(8,128)} %all-reduce.13.cloned.1.call-done) | copy-start | bytes 1966084
  783.1 476.9 %all-reduce.17.cloned.1.call-start = ((), (), s32[]{:S(2)}) async-start(), calls=%async_computation.4 | async-start | bytes 655360
  917.7 1.0 copy-start.4
  1260.7 23.7 %collective-permute-start.2 = (bf16[4,1,640]{2,1,0:T(2,128)(2,1)S(1)}, bf16[4,1,640]{2,1,0:T(2,128)(2,1)S(1)}, u32[]{:S(2)}, u32[]{:S(2)}) collective-permute-start(bf16[4,1,640]{2,1,0:T(2,128)(2,1)S(1)} %get-tuple-element.120), channel_id=1, source_target_pairs={{0,32},{32,64},{64,96},{96,128},{128,160},{160,192},{192,224},{224... | collective-permute-start | bytes 15368 | tf_op jit(solution)/shard_map/ppermute | solution.py:21
  1282.4 5.0 collective-permute-start.3
  1284.4 3.1 copy-start.7
  1284.4 3.1 copy-start.9
  1284.4 3.1 copy-start.11
  1288.4 6.6 collective-permute-start
  1290.3 5.9 collective-permute-start.1
  1298.8 7.4 collective-permute-start
  1300.7 6.6 collective-permute-start.1
  1310.0 7.4 collective-permute-start
  1311.9 6.6 collective-permute-start.1
  1321.1 7.4 collective-permute-start
  1323.1 6.6 collective-permute-start.1
  (3 other events, 1.9 us)
Sparse Core Ops, SparseCore 0:
  11.1 278.3 all-reduce.8
  292.8 134.1 all-reduce.10
  505.7 274.7 all-reduce.12
  783.4 134.1 all-reduce.14
  996.2 263.7 all-reduce.16
where the time goes:
time: 1340 us
  waiting for transfers between devices  1100 us (82%)
  blocking collectives  103 us (8%)
  other arithmetic  51 us (4%)
  starting transfers between devices  48.5 us (4%)
  matrix products  16.5 us (1%)
  between operations  14.7 us (1%)
    psum x2, waiting for transfers between devices, shards(): basis = lax.psum(inner(frames, omega), 'frame')  553 us
    psum x2, waiting for transfers between devices, shards(): ortho = orthonormal(basis, lax.psum(inner(basis, basis), 'pix'))  268 us
    unnamed x6, waiting for transfers between devices  262 us
    psum x2, blocking collectives, shards(): coeffs = lax.psum(product(frames, ortho), 'pix')  103 us
    ppermute x5, starting transfers between devices, extended_2(): before = lax.ppermute(last, axis, up)  38.5 us
  transfers between devices with their start and end apart: 15, of which 14 were waited for; matrix products, arithmetic and copies ran while one was open for 0% of the time, Pallas kernels for 0%

commit v1 on v0

v1 whole, which is shorter than its diff:
```python
import jax
import jax.numpy as jnp
from jax import lax
from jax.experimental import pallas as pl
from jax.experimental.pallas import tpu as pltpu
from jax.sharding import PartitionSpec as P

MESH = pl.DeviceIdType.MESH
F32 = jnp.float32
BF16 = jnp.bfloat16

W = 640
RANK = 128
HID = 64
NZ = 16
NP = 16
FB = 64
PXH = 40
PX = 2 * PXH
FH = NZ * FB
THRESHOLD = 0.5


def dot(a, b):
    return lax.dot_general(
        a, b, (((1,), (0,)), ((), ())), precision=lax.Precision.HIGHEST, preferred_element_type=F32
    )


def dot_nt(a, b):
    return lax.dot_general(
        a, b, (((1,), (1,)), ((), ())), precision=lax.Precision.HIGHEST, preferred_element_type=F32
    )


def iota(shape, dim):
    return lax.broadcasted_iota(jnp.int32, shape, dim)


BLOCK = 32


def start_factor(work, gram):
    work[:, 0:RANK] = gram
    work[:, RANK : 2 * RANK] = (iota((RANK, RANK), 0) == iota((RANK, RANK), 1)).astype(F32)


def eliminate(work, result, first, last):
    tiles = BLOCK // 8
    row_in_tile = iota((8, 128), 0)

    def one(number, carry):
        left = [work[8 * t : 8 * t + 8, 0:RANK] for t in range(tiles)]
        right = [work[8 * t : 8 * t + 8, RANK:] for t in range(tiles)]
        columns = [
            [jnp.broadcast_to(left[t][:, m : m + 1], (8, 128)) for t in range(tiles)]
            for m in range(BLOCK)
        ]
        pivots = []
        for j in range(BLOCK):
            t0, r0 = j // 8, j % 8

            def row_of(tile):
                return jnp.broadcast_to(tile[r0 : r0 + 1, :], (8, 128))

            pivot = row_of(columns[j][t0])
            pivots.append(pivot)
            scale = 1.0 / pivot
            factors = [columns[j][t] * scale for t in range(tiles)]
            factors[t0] = jnp.where(row_in_tile > r0, factors[t0], 0.0)
            for m in range(j + 1, BLOCK):
                value = row_of(columns[m][t0])
                for t in range(t0, tiles):
                    columns[m][t] = columns[m][t] - factors[t] * value
            left_row, right_row = row_of(left[t0]), row_of(right[t0])
            for t in range(t0, tiles):
                left[t] = left[t] - factors[t] * left_row
                right[t] = right[t] - factors[t] * right_row
        for t in range(tiles):
            own = pivots[8 * t]
            for r in range(1, 8):
                own = jnp.where(row_in_tile == r, pivots[8 * t + r], own)
            scale = 1.0 / jnp.sqrt(own)
            left[t] = left[t] * scale
            right[t] = right[t] * scale
        left = jnp.concatenate(left, axis=0)
        right = jnp.concatenate(right, axis=0)
        result[pl.ds(pl.multiple_of(number * BLOCK, BLOCK), BLOCK), :] = right

        @pl.when(number < RANK // BLOCK - 1)
        def _():
            across = left.T[BLOCK:, :]
            rest = work[BLOCK:, 0:RANK] - dot(across, left)
            work[0 : RANK - BLOCK, 0:RANK] = pltpu.roll(rest, RANK - BLOCK, 1)
            work[0 : RANK - BLOCK, RANK:] = work[BLOCK:, RANK:] - dot(across, right)

        return carry

    lax.fori_loop(first, last, one, 0)


def push(src, dst, send, recv, device):
    pltpu.make_async_remote_copy(
        src_ref=src, dst_ref=dst, send_sem=send, recv_sem=recv,
        device_id={"frame": device[0], "pix": device[1]}, device_id_type=MESH,
    ).start()


def parts(x, count):
    out = []
    for _ in range(count):
        out.append(x.astype(BF16))
        x = x - out[-1].astype(F32)
    return out


def bdot(a, b):
    return jnp.dot(a, b, preferred_element_type=F32)


RING = (8, 7, 9, 6, 10, 5, 11, 4, 12, 3, 13, 2, 14, 1, 15)
EIGHTHS = (4, 2, 6, 5, 3, 7, 1)


def each(distances, send):
    for d in distances:
        send(d)


def drain(ref, sem):
    pltpu.make_async_copy(ref, ref, sem).wait()


def kernel(
    frames_hbm, basis0, picks_hbm, bias_in_hbm, conv_in, conv_out, bias_out,
    coeffs_out, scores_out,
    frames, picks, bias_in, t_buf, r_buf, om, at, an, sel_t, sel, xs, xr, ss, sr,
    s1, c1, t1, r1, k1, zy1, kg1, zg1, yz, yf, gf,
    s2, r2, k2, zy2, sg, rg, kg2, zg2, ft, fy,
    work, linv, slab, slabs, image, halo, taps, w1, w2, bias_wide,
    send, recv, load, arrive, came,
):
    group = lax.axis_index("frame")
    pix = lax.axis_index("pix")
    half = group // NZ
    z = group % NZ
    base = half * NZ
    q = pix // 2
    c = pix % 2
    fetch = pltpu.make_async_copy(frames_hbm, frames, load.at[0])
    fetch.start()
    fetch_picks = pltpu.make_async_copy(picks_hbm, picks, load.at[2])
    fetch_picks.start()
    fetch_bias = pltpu.make_async_copy(bias_in_hbm, bias_in, load.at[3])
    fetch_bias.start()

    across_group = (1 - half) * NZ + z
    partner = (across_group, pix)
    other_core = (group, 2 * q + 1 - c)
    wrap = lax.rem

    barrier = pltpu.get_barrier_semaphore()

    def greet(d):
        to = wrap(pix + d, NP)
        for frame, at_pix in ((base + wrap(z + d, NZ), pix), (group, to), (across_group, to)):
            pl.semaphore_signal(
                barrier, inc=1, device_id={"frame": frame, "pix": at_pix}, device_id_type=MESH
            )

    each(RING, greet)
    pl.semaphore_signal(
        barrier, inc=1, device_id={"frame": across_group, "pix": pix}, device_id_type=MESH
    )

    fetch.wait()
    both = jnp.concatenate([frames[:, 0:W], frames[:, W : 2 * W]], axis=0)
    for t in range(5):
        tile = both[:, 128 * t : 128 * t + 128].T
        for lo in range(128 * t, 128 * t + 128, 8):
            t_buf[lo // PXH, lo % PXH : lo % PXH + 8, :] = tile[lo - 128 * t : lo - 128 * t + 8, :]

    pl.semaphore_wait(barrier, 46)

    eighth = pl.multiple_of(q * 8, 8)

    def send_basis(d):
        push(
            basis0.at[pl.ds(eighth, 8)], om.at[z, q], send.at[0], recv.at[0],
            (base + wrap(z + d, NZ), pix),
        )

    def send_frames(d):
        to = wrap(z + d, NZ)
        push(t_buf.at[to], r_buf.at[z], send.at[1], came.at[z], (base + to, pix))

    each(RING, send_basis)
    each(RING[:9], send_frames)
    own_part = pltpu.make_async_copy(basis0.at[pl.ds(eighth, 8)], om.at[z, q], load.at[1])
    own_part.start()
    r_buf[z] = t_buf[z]
    own_part.wait()

    up = (iota((4 * HID, HID), 0) % HID == iota((4 * HID, HID), 1))
    wide = (iota((9, 72), 1) // 8 == iota((9, 72), 0))
    same = iota((4 * HID, 72), 0) // HID == iota((4 * HID, 72), 1) % 8
    spread = lax.dot_general(
        conv_in[...], wide.astype(BF16), (((0,), (0,)), ((), ())), preferred_element_type=F32
    ).astype(BF16)
    spread = jnp.dot(up.astype(BF16), spread, preferred_element_type=F32)
    w1[...] = jnp.where(same, spread, 0.0).astype(BF16)
    tall = (iota((72, 9), 0) // 8 == iota((72, 9), 1))
    over = (iota((HID, 4 * HID), 1) % HID == iota((HID, 4 * HID), 0))
    same = iota((72, 4 * HID), 1) // HID == iota((72, 4 * HID), 0) % 8
    spread = jnp.dot(tall.astype(BF16), conv_out[...], preferred_element_type=F32).astype(BF16)
    spread = jnp.dot(spread, over.astype(BF16), preferred_element_type=F32)
    w2[...] = jnp.where(same, spread, 0.0).astype(BF16)
    fetch_bias.wait()
    fetch_picks.wait()
    bias_wide[...] = dot_nt(up.astype(F32), jnp.broadcast_to(bias_in[...], (128, HID)))
    taps[...] = jnp.zeros_like(taps)

    drain(om.at[pl.ds(0, NZ - 1), 0], recv.at[0])

    def spread_basis(d):
        push(om.at[:, q], om.at[:, q], send.at[2], recv.at[2], (group, 2 * wrap(q + d, 8) + c))

    for d in EIGHTHS:
        spread_basis(d)
        each(RING[8 + EIGHTHS.index(d) : 9 + EIGHTHS.index(d)] if d != EIGHTHS[0] else (), send_frames)

    low = iota((PXH, 128), 1) < FB
    for k in (4, 3, 5, 2, 6, 1, 7, 0):
        m = wrap(z // 2 + k, NZ // 2)
        if k:
            drain(r_buf.at[2 * m], came.at[2 * m])
            drain(r_buf.at[2 * m + 1], came.at[2 * m + 1])
        else:
            other = 2 * m + 1 - z % 2
            drain(r_buf.at[other], came.at[other])
        first, second = r_buf[2 * m], r_buf[2 * m + 1]
        tile = jnp.concatenate(
            [
                jnp.where(low, first, pltpu.roll(second, FB, 1)),
                jnp.where(low, pltpu.roll(first, FB, 1), second),
            ],
            axis=0,
        )
        at[:, pl.ds(pl.multiple_of(128 * m, 128), 128)] = jnp.concatenate(parts(tile, 3), axis=0)

    def frames_times(x):
        out = bdot(at[...], jnp.concatenate(parts(x, 2), axis=1))
        out = out[:, 0:RANK] + out[:, RANK:]
        return out[0:PX] + (out[PX : 2 * PX] + out[2 * PX :])

    def rows_times(x):
        hi, lo = parts(x, 2)
        return bdot(an[...], jnp.concatenate([hi, hi, lo], axis=0))

    drain(om.at[:, pl.ds(0, 7)], recv.at[2])
    xs[0] = frames_times(om[...].reshape(FH, RANK))
    push(xs.at[0], xr.at[0], send.at[4], recv.at[4], partner)

    chosen_here = (iota((FH, 128), 0) + half * FH == picks[...]).astype(BF16)
    out = bdot(at[...], chosen_here)
    ss[...] = out[0:PX] + (out[PX : 2 * PX] + out[2 * PX :])
    push(ss, sr, send.at[3], recv.at[3], partner)
    for m in range(NZ // 2):
        tile = at[0 : 2 * PX, 128 * m : 128 * m + 128].astype(F32)
        tile = jnp.concatenate([tile, tile[0:PX]], axis=0)
        an[128 * m : 128 * m + 128, :] = tile.T.astype(BF16)
    drain(xr.at[0], recv.at[4])

    def to_pix(out, got, sem):
        def send_pix(d):
            to = wrap(pix + d, NP)
            push(out.at[to], got.at[pix], send.at[sem], recv.at[sem], (group, to))

        each(RING, send_pix)
        got[pix] = out[pix]

    def all_pix(buffer, sem):
        def send_pix(d):
            push(buffer.at[pix], buffer.at[pix], send.at[sem], recv.at[sem], (group, wrap(pix + d, NP)))

        each(RING, send_pix)

    def total(buffer, sem):
        drain(buffer.at[pl.ds(0, 15)], recv.at[sem])
        value = buffer[0]
        for s in range(1, 16):
            value = value + buffer[s]
        return value

    def tiles_to_z(packed, landed, sem):
        def send_z(d):
            to = wrap(z + d, NZ)
            push(packed.at[to % 8], landed.at[z], send.at[sem], recv.at[sem], (base + to, pix))

        each(RING, send_z)
        landed[z] = packed[z % 8]

    def same_to_z(packed, landed, sem):
        def send_z(d):
            push(packed, landed.at[z], send.at[sem], recv.at[sem], (base + wrap(z + d, NZ), pix))

        each(RING, send_z)
        landed[z] = packed[...]

    basis = xs[0] + xr[0]
    y = rows_times(basis)
    for qq in range(8):
        for cc in range(2):
            for k in range(8):
                row = FB * (8 * cc + k) + 8 * qq
                s1[cc, qq, k] = y[row : row + 8, :]
    gram = dot(basis.T, basis)
    for tile in range(NP):
        s1[tile % 2, tile // 2, 8] = gram[8 * tile : 8 * tile + 8, :]
    push(s1.at[1 - c], c1, send.at[5], recv.at[5], other_core)
    drain(sr, recv.at[3])
    sel_t[...] = ss[...] + sr[...]
    sel[...] = sel_t[...].T
    drain(c1, recv.at[5])
    for qq in range(8):
        t1[qq] = s1[c, qq] + c1[qq]

    def send_eighths(d):
        to = wrap(q + d, 8)
        push(t1.at[to], r1.at[q], send.at[21], recv.at[21], (group, 2 * to + c))

    each(EIGHTHS, send_eighths)
    r1[q] = t1[q]
    drain(r1.at[pl.ds(0, 7)], recv.at[21])
    value = r1[0]
    for s in range(1, 8):
        value = value + r1[s]
    k1[...] = value[0:8]
    kg1[...] = value[8]
    tiles_to_z(k1, zy1, 6)
    same_to_z(kg1, zg1, 17)
    yz[z % 8] = total(zy1, 6)
    for d in (4, -3, 3, -2, 2, -1, 1):
        push(
            yz.at[z % 8], yz.at[z % 8], send.at[7], recv.at[7],
            (base + wrap(z + (d + NZ) % NZ, NZ), pix),
        )
    gf[pix] = total(zg1, 17)
    all_pix(gf, 8)
    drain(yz.at[pl.ds(0, 7)], recv.at[7])
    ours, theirs = pl.ds(8 * c, 8), pl.ds(8 * (1 - c), 8)
    for d in EIGHTHS:
        push(
            yz, yf.at[ours, q], send.at[9], arrive.at[d], (group, 2 * wrap(q + d, 8) + c)
        )
    yf[ours, q] = yz[...]
    push(yf.at[ours, q], yf.at[ours, q], send.at[22], recv.at[22], other_core)
    drain(gf.at[pl.ds(0, NP - 1)], recv.at[8])
    start_factor(work, gf[...].reshape(RANK, RANK))
    eliminate(work, linv, 0, 2)
    for d in EIGHTHS:
        origin = wrap(q + 8 - d, 8)
        drain(yf.at[ours, origin], arrive.at[d])
        push(yf.at[ours, origin], yf.at[ours, origin], send.at[22], recv.at[22], other_core)
    eliminate(work, linv, 2, 3)
    drain(yf.at[theirs], recv.at[22])

    xs[1] = frames_times(yf[...].reshape(FH, RANK))
    push(xs.at[1], xr.at[1], send.at[10], recv.at[10], partner)
    eliminate(work, linv, 3, 4)
    drain(xr.at[1], recv.at[10])
    basis = dot_nt(xs[1] + xr[1], linv[...])
    across = basis.T
    sg[...] = dot(jnp.where(half == 0, across, sel[...]), basis).reshape(NP, 8, RANK)
    to_pix(sg, rg, 11)
    y = rows_times(basis)
    for owner in range(NP):
        for k in range(8):
            row = FB * (8 * (owner % 2) + k) + 8 * (owner // 2)
            s2[owner, k] = y[row : row + 8, :]
    kg2[...] = total(rg, 11)
    same_to_z(kg2, zg2, 13)
    to_pix(s2, r2, 12)
    place = half * NP + pix
    ft[place] = total(zg2, 13)

    def send_both(d):
        to = wrap(pix + d, NP)
        push(ft.at[place], ft.at[place], send.at[18], recv.at[18], (group, to))
        push(ft.at[place], ft.at[place], send.at[18], recv.at[18], (across_group, to))

    push(ft.at[place], ft.at[place], send.at[18], recv.at[18], partner)
    each(RING, send_both)
    k2[...] = total(r2, 12)
    tiles_to_z(k2, zy2, 19)
    drain(ft.at[pl.ds(0, 2 * NP - 1)], recv.at[18])
    start_factor(work, ft[0:NP].reshape(RANK, RANK))
    eliminate(work, linv, 0, 3)
    fy[pix] = total(zy2, 19)
    all_pix(fy, 20)
    eliminate(work, linv, 3, 4)

    own = dot_nt(ft[pl.ds(NP + 8 * half, 8)].reshape(FB, RANK), linv[...])
    ortho_t = dot(linv[...], across)
    chosen = sel[pl.ds(pl.multiple_of(FB * half, FB), FB), :] - dot(own, ortho_t)
    shrunk = jnp.where(
        chosen > THRESHOLD,
        chosen - THRESHOLD,
        jnp.where(chosen < -THRESHOLD, chosen + THRESHOLD, 0.0),
    )
    shrunk = shrunk.astype(BF16).astype(F32)
    shrunk = jnp.concatenate([shrunk, jnp.zeros((FB, 128 - PX), F32)], axis=1)
    for t in range(NZ):
        slab[t] = shrunk[4 * t : 4 * t + 4, :]

    def send_slab(d):
        to = wrap(z + d, NZ)
        push(slab.at[to], slabs.at[z], send.at[14], recv.at[14], (base + to, pix))

    each(RING, send_slab)
    slabs[z] = slab[z]
    drain(fy.at[pl.ds(0, NP - 1)], recv.at[20])
    upper = z >= 8
    mine = [jnp.where(upper, fy[2 * k + 1], fy[2 * k]) for k in range(8)]
    coeffs_out[...] = dot_nt(jnp.concatenate(mine, axis=0), linv[...])
    drain(slabs.at[pl.ds(0, NZ - 1)], recv.at[14])

    lane = iota((4, 128), 1)
    strips = []
    for row in range(2):
        tiles = [jnp.zeros((4, 128), F32) for _ in range(5)]
        for t in range(NZ):
            at_tile, shift = (PXH * t) // 128, (PXH * t) % 128
            piece = slabs[t]
            turn = (shift - PXH * row) % 128
            if turn:
                piece = pltpu.roll(piece, turn, 1)
            tiles[at_tile] = jnp.where((lane >= shift) & (lane < shift + PXH), piece, tiles[at_tile])
            if shift + PXH > 128:
                tiles[at_tile + 1] = jnp.where(lane < shift + PXH - 128, piece, tiles[at_tile + 1])
        strips.append(jnp.concatenate(tiles, axis=1))
    image[...] = jnp.concatenate(strips, axis=0)

    push(image, halo.at[0], send.at[15], recv.at[15], (group, wrap(pix + 1, NP)))
    push(image, halo.at[1], send.at[16], recv.at[16], (group, wrap(pix + NP - 1, NP)))
    drain(halo.at[0], recv.at[15])
    drain(halo.at[1], recv.at[16])
    first, last = pix == 0, pix == NP - 1
    above = jnp.where(first, 0.0, halo[0])
    below = jnp.where(last, 0.0, halo[1])
    here = image[...]
    rows = [above[0:4], above[4:8], here[0:4], here[4:8], below[0:4], below[4:8]]
    place_in_row = iota((4, W), 1)
    for b in range(3):
        for k, row in enumerate(rows):
            if b == 0:
                row = jnp.where(place_in_row == 0, 0.0, pltpu.roll(row, 1, 1))
            elif b == 2:
                row = jnp.where(place_in_row == W - 1, 0.0, pltpu.roll(row, W - 1, 1))
            for a in range(3):
                h = k - a
                if 0 <= h < 4:
                    tap = 3 * a + b
                    taps[8 * tap : 8 * tap + 4, W * h : W * h + W] = row
    bias = jnp.concatenate([bias_wide[...]] * 5, axis=1)
    layers = []
    for h in range(4):
        hidden = jnp.dot(
            w1[...], taps[:, W * h : W * h + W].astype(BF16), preferred_element_type=F32
        )
        hidden = jnp.maximum(hidden + bias, 0.0)
        if h == 0:
            hidden = jnp.where(first, 0.0, hidden)
        if h == 3:
            hidden = jnp.where(last, 0.0, hidden)
        layers.append(jnp.dot(w2[...], hidden.astype(BF16), preferred_element_type=F32))
    for r in range(2):
        summed = jnp.broadcast_to(bias_out[...], (4, W))
        for b in range(3):
            part = sum(layers[r + a][8 * (3 * a + b) : 8 * (3 * a + b) + 4, :] for a in range(3))
            if b == 0:
                part = jnp.where(place_in_row == 0, 0.0, pltpu.roll(part, 1, 1))
            elif b == 2:
                part = jnp.where(place_in_row == W - 1, 0.0, pltpu.roll(part, W - 1, 1))
            summed = summed + part
        scores_out[:, W * r : W * r + W] = summed

    drain(om.at[pl.ds(0, NZ - 1), 0], send.at[0])
    drain(t_buf.at[pl.ds(0, NZ - 1)], send.at[1])
    drain(om.at[:, pl.ds(0, 7)], send.at[2])
    drain(ss, send.at[3])
    drain(xs.at[0], send.at[4])
    drain(c1, send.at[5])
    drain(r1.at[pl.ds(0, 7)], send.at[21])
    drain(yf.at[theirs], send.at[22])
    drain(zy1.at[pl.ds(0, NZ - 1)], send.at[6])
    drain(yz.at[pl.ds(0, 7)], send.at[7])
    drain(gf.at[pl.ds(0, NP - 1)], send.at[8])
    drain(yf.at[pl.ds(0, 7)], send.at[9])
    drain(xs.at[1], send.at[10])
    drain(sg.at[pl.ds(0, NP - 1)], send.at[11])
    drain(s2.at[pl.ds(0, NP - 1)], send.at[12])
    drain(zg2.at[pl.ds(0, NZ - 1)], send.at[13])
    drain(zg1.at[pl.ds(0, NZ - 1)], send.at[17])
    drain(ft.at[pl.ds(0, 2 * NP - 1)], send.at[18])
    drain(zy2.at[pl.ds(0, NZ - 1)], send.at[19])
    drain(fy.at[pl.ds(0, NP - 1)], send.at[20])
    drain(slab.at[pl.ds(0, NZ - 1)], send.at[14])
    drain(image, send.at[15])
    drain(image, send.at[16])


def shards(frames, start_basis, picks, conv_in, bias_in, conv_out, bias_out):
    vmem = pltpu.VMEM
    scratch = [
        vmem((FB, 2 * W), F32),
        vmem((1, 128), jnp.int32),
        vmem((1, HID), F32),
        vmem((NZ, PXH, 128), F32),
        vmem((NZ, PXH, 128), F32),
        vmem((NZ, 8, 8, RANK), F32),
        vmem((3 * PX, FH), BF16),
        vmem((FH, 3 * PX), BF16),
        vmem((PX, 128), F32),
        vmem((128, PX), F32),
        vmem((2, PX, RANK), F32),
        vmem((2, PX, RANK), F32),
        vmem((PX, 128), F32),
        vmem((PX, 128), F32),
        vmem((2, 8, 9, 8, RANK), F32),
        vmem((8, 9, 8, RANK), F32),
        vmem((8, 9, 8, RANK), F32),
        vmem((8, 9, 8, RANK), F32),
        vmem((8, 8, RANK), F32),
        vmem((NZ, 8, RANK), F32),
        vmem((8, RANK), F32),
        vmem((NZ, 8, RANK), F32),
        vmem((8, 8, RANK), F32),
        vmem((NZ, 8, 8, RANK), F32),
        vmem((NP, 8, RANK), F32),
        vmem((NP, 8, 8, RANK), F32),
        vmem((NP, 8, 8, RANK), F32),
        vmem((8, 8, RANK), F32),
        vmem((NZ, 8, RANK), F32),
        vmem((NP, 8, RANK), F32),
        vmem((NP, 8, RANK), F32),
        vmem((8, RANK), F32),
        vmem((NZ, 8, RANK), F32),
        vmem((2 * NP, 8, RANK), F32),
        vmem((NP, 8, RANK), F32),
        vmem((RANK, 2 * RANK), F32),
        vmem((RANK, RANK), F32),
        vmem((NZ, 4, 128), F32),
        vmem((NZ, 4, 128), F32),
        vmem((8, W), F32),
        vmem((2, 8, W), F32),
        vmem((72, 4 * W), F32),
        vmem((4 * HID, 72), BF16),
        vmem((72, 4 * HID), BF16),
        vmem((4 * HID, 128), F32),
        pltpu.SemaphoreType.DMA((23,)),
        pltpu.SemaphoreType.DMA((23,)),
        pltpu.SemaphoreType.DMA((4,)),
        pltpu.SemaphoreType.DMA((8,)),
        pltpu.SemaphoreType.DMA((NZ,)),
    ]
    whole = pl.BlockSpec(memory_space=pltpu.VMEM)
    return pl.pallas_call(
        kernel,
        out_shape=(
            jax.ShapeDtypeStruct((FB, RANK), F32),
            jax.ShapeDtypeStruct((4, 2 * W), F32),
        ),
        in_specs=[pl.BlockSpec(memory_space=pltpu.HBM)] * 4 + [whole] * 3,
        out_specs=(whole, whole),
        scratch_shapes=scratch,
        compiler_params=pltpu.CompilerParams(
            collective_id=0, has_side_effects=True, vmem_limit_bytes=64 * 1024 * 1024
        ),
        cost_estimate=pl.CostEstimate(
            flops=1_500_000_000, bytes_accessed=1_000_000, transcendentals=0
        ),
    )(
        frames,
        start_basis,
        picks.reshape(1, 128),
        bias_in.reshape(1, HID),
        conv_in.T,
        conv_out,
        bias_out.reshape(1, 1),
    )


def solution(mesh):
    placed = (P("frame", "pix"), P("frame", None), P(), P(), P(), P(), P())
    return jax.shard_map(
        shards,
        mesh=mesh,
        in_specs=placed,
        out_specs=(P("frame", None), P("frame", "pix")),
        check_vma=False,
    )
```

time: 1340 us -> 108 us (0.08)
  waiting for transfers between devices: 1100 us -> 0 us
  Pallas kernels: 0 us -> 105 us
  blocking collectives: 103 us -> 0 us
  other arithmetic: 51 us -> 0 us
  starting transfers between devices: 48.5 us -> 0 us
  matrix products: 16.5 us -> 0 us
    psum x4 -> x0, waiting for transfers between devices: 822 us -> none  [the longest x2 553 us: shards(): basis = lax.psum(inner(frames, omega), 'frame')]
    unnamed x6 -> x0, waiting for transfers between devices: 262 us -> none
    pallas_call x0 -> x1, Pallas kernels: none -> 105 us  [shards(): pl.pallas_call(kernel, out_shape=(jax.ShapeDtypeStruct((FB, RANK), F32),...]
    psum x2 -> x0, blocking collectives: 103 us -> none  [shards(): coeffs = lax.psum(product(frames, ortho), 'pix')]
    ppermute x10 -> x0, starting transfers between devices: 48.1 us -> none  [the longest x5 38.5 us: extended_2(): before = lax.ppermute(last, axis, up)]
    another operation x10 -> x0, other arithmetic: 45.7 us -> none  [the longest x6 24.8 us: orthonormal(): return solve_factor(jnp.linalg.cholesky(gram), block)]
    dot_general x16 -> x0, matrix products: 15 us -> none  [the longest x4 10.3 us: inner(): lax.dot_general(left, right, (((0,), (0,)), ((), ())), precision=lax.Prec...]
  transfers between devices with their start and end apart: 15 -> 0, of which waited for: 14 -> 0; matrix products, arithmetic and copies ran while one was open for 0% -> 0% of each run, Pallas kernels for 0% -> 0%
where the time goes in v1:
time: 108 us
  Pallas kernels  105 us (97%)
  local copies, waits for them, and re-layouts  1.99 us (2%)
  between operations  1.3 us (1%)
    pallas_call x1, Pallas kernels, shards(): pl.pallas_call(kernel, out_shape=(jax.ShapeDtypeStruct((FB, RANK), F32),...  105 us

profile of v1, /device:TPU:1, one launch (start us, length us, event | category | flops | bytes accessed | tf_op | source)
XLA Modules:
  0.0 108.0 jit_solution(1302818922926014387)
XLA Ops:
  1.3 104.7 %shard_map.86 = (f32[64,128]{1,0:T(8,128)}, f32[4,1280]{1,0:T(4,128)}) custom-call(f32[64,1280]{1,0:T(8,128)} %frames_hbm.1, f32[64,128]{1,0:T(8,128)} %basis0.1, s32[1,128]{1,0:T(1,128)} %bitcast.6, f32[1,64]{1,0:T(1,128)} %bitcast.7, bf16[9,64]{1,0:T(8,128)(2,1)} %bitcast.5, bf16[9,64]{1,0:T(8,128)(2,1)} %conv_out.1, f32[1,1]{1,0:T(1,128)} %bitcast.4.bias_out), custom_call_target="tpu_custom_call" | custom-call | flops 1500000000 | bytes 1000000 | tf_op jit(solution)/shard_map/pallas_call | solution.py:568
  106.0 0.0 copy-start
  106.0 1.4 %copy.12 = f32[64,128]{1,0:T(8,128)} copy(f32[64,128]{1,0:T(8,128)} %get-tuple-element.4) | data formatting | bytes 65536
  107.4 0.0 copy-done
  107.4 0.6 copy.13
Async XLA Ops:
  106.0 1.4 %copy-start = (f32[4,1280]{1,0:T(4,128)S(1)}, f32[4,1280]{1,0:T(4,128)}, u32[]{:S(2)}) copy-start(f32[4,1280]{1,0:T(4,128)} %get-tuple-element.5) | copy-start | bytes 61444

commit v2 on v1

--- a/solution.py
+++ b/solution.py
@@ -41,8 +41,12 @@
 
 
 def start_factor(work, gram):
-    work[:, 0:RANK] = gram
-    work[:, RANK : 2 * RANK] = (iota((RANK, RANK), 0) == iota((RANK, RANK), 1)).astype(F32)
+    diagonal = iota((RANK, RANK), 0) == iota((RANK, RANK), 1)
+    own = jnp.where(diagonal, gram, 0.0)
+    by_row = 1.0 / jnp.sqrt(jnp.sum(own, axis=1, keepdims=True))
+    by_column = 1.0 / jnp.sqrt(jnp.sum(own, axis=0, keepdims=True))
+    work[:, 0:RANK] = gram * by_row * by_column
+    work[:, RANK : 2 * RANK] = jnp.where(diagonal, by_column, 0.0)
 
 
 def eliminate(work, result, first, last):
@@ -57,25 +61,36 @@
             for m in range(BLOCK)
         ]
         pivots = []
-        for j in range(BLOCK):
+        for j in range(0, BLOCK, 2):
             t0, r0 = j // 8, j % 8
 
-            def row_of(tile):
-                return jnp.broadcast_to(tile[r0 : r0 + 1, :], (8, 128))
-
-            pivot = row_of(columns[j][t0])
-            pivots.append(pivot)
-            scale = 1.0 / pivot
-            factors = [columns[j][t] * scale for t in range(tiles)]
-            factors[t0] = jnp.where(row_in_tile > r0, factors[t0], 0.0)
-            for m in range(j + 1, BLOCK):
-                value = row_of(columns[m][t0])
+            def row_of(tile, r):
+                return jnp.broadcast_to(tile[r : r + 1, :], (8, 128))
+
+            one_, cross = row_of(columns[j][t0], r0), row_of(columns[j + 1][t0], r0)
+            two = row_of(columns[j + 1][t0], r0 + 1)
+            det = one_ * two - cross * cross
+            over_one = 1.0 / one_
+            over_two = one_ * (1.0 / det)
+            link = cross * over_one
+            pivots += [one_, det * over_one]
+            first, second = {}, {}
+            for t in range(t0, tiles):
+                first[t] = columns[j][t] * over_one
+                second[t] = (columns[j + 1][t] - link * columns[j][t]) * over_two
+            first[t0] = jnp.where(row_in_tile > r0 + 1, first[t0], 0.0)
+            second[t0] = jnp.where(row_in_tile > r0 + 1, second[t0], 0.0)
+            for m in range(j + 2, BLOCK):
+                upper = row_of(columns[m][t0], r0)
+                lower = row_of(columns[m][t0], r0 + 1) - link * upper
                 for t in range(t0, tiles):
-                    columns[m][t] = columns[m][t] - factors[t] * value
-            left_row, right_row = row_of(left[t0]), row_of(right[t0])
-            for t in range(t0, tiles):
-                left[t] = left[t] - factors[t] * left_row
-                right[t] = right[t] - factors[t] * right_row
+                    columns[m][t] = columns[m][t] - (first[t] * upper + second[t] * lower)
+            for side in (left, right):
+                upper = row_of(side[t0], r0)
+                lower = row_of(side[t0], r0 + 1) - link * upper
+                for t in range(t0, tiles):
+                    side[t] = side[t] - (first[t] * upper + second[t] * lower)
+                side[t0] = jnp.where(row_in_tile == r0 + 1, lower, side[t0])
         for t in range(tiles):
             own = pivots[8 * t]
             for r in range(1, 8):
@@ -137,7 +152,7 @@
     frames, picks, bias_in, t_buf, r_buf, om, at, an, sel_t, sel, xs, xr, ss, sr,
     s1, c1, t1, r1, k1, zy1, kg1, zg1, yz, yf, gf,
     s2, r2, k2, zy2, sg, rg, kg2, zg2, ft, fy,
-    work, linv, slab, slabs, image, halo, taps, w1, w2, bias_wide,
+    work, linv, slab, slabs, near, bs, selx, across_x, taps, w1, w2, bias_wide,
     send, recv, load, arrive, came,
 ):
     group = lax.axis_index("frame")
@@ -194,12 +209,21 @@
         to = wrap(z + d, NZ)
         push(t_buf.at[to], r_buf.at[z], send.at[1], came.at[z], (base + to, pix))
 
-    each(RING, send_basis)
+    carries = c == z // 8
+
+    @pl.when(carries)
+    def _():
+        each(RING, send_basis)
+
     each(RING[:9], send_frames)
-    own_part = pltpu.make_async_copy(basis0.at[pl.ds(eighth, 8)], om.at[z, q], load.at[1])
-    own_part.start()
+
+    @pl.when(carries)
+    def _():
+        own_part = pltpu.make_async_copy(basis0.at[pl.ds(eighth, 8)], om.at[z, q], load.at[1])
+        own_part.start()
+        own_part.wait()
+
     r_buf[z] = t_buf[z]
-    own_part.wait()
 
     up = (iota((4 * HID, HID), 0) % HID == iota((4 * HID, HID), 1))
     wide = (iota((9, 72), 1) // 8 == iota((9, 72), 0))
@@ -220,14 +244,24 @@
     bias_wide[...] = dot_nt(up.astype(F32), jnp.broadcast_to(bias_in[...], (128, HID)))
     taps[...] = jnp.zeros_like(taps)
 
-    drain(om.at[pl.ds(0, NZ - 1), 0], recv.at[0])
+    @pl.when(carries)
+    def _():
+        drain(om.at[pl.ds(0, 7), 0], recv.at[0])
+
+    @pl.when(c != z // 8)
+    def _():
+        drain(om.at[pl.ds(0, 8), 0], recv.at[0])
+
+    lower_z = pl.ds(8 * c, 8)
 
     def spread_basis(d):
-        push(om.at[:, q], om.at[:, q], send.at[2], recv.at[2], (group, 2 * wrap(q + d, 8) + c))
-
-    for d in EIGHTHS:
+        push(
+            om.at[lower_z, q], om.at[lower_z, q], send.at[2], recv.at[2], (group, wrap(pix + d, NP))
+        )
+
+    for n, d in enumerate(RING):
         spread_basis(d)
-        each(RING[8 + EIGHTHS.index(d) : 9 + EIGHTHS.index(d)] if d != EIGHTHS[0] else (), send_frames)
+        each(RING[9 + n : 10 + n], send_frames)
 
     low = iota((PXH, 128), 1) < FB
     for k in (4, 3, 5, 2, 6, 1, 7, 0):
@@ -257,7 +291,7 @@
         hi, lo = parts(x, 2)
         return bdot(an[...], jnp.concatenate([hi, hi, lo], axis=0))
 
-    drain(om.at[:, pl.ds(0, 7)], recv.at[2])
+    drain(om.at[pl.ds(0, 15)], recv.at[2])
     xs[0] = frames_times(om[...].reshape(FH, RANK))
     push(xs.at[0], xr.at[0], send.at[4], recv.at[4], partner)
 
@@ -308,29 +342,36 @@
         landed[z] = packed[...]
 
     basis = xs[0] + xr[0]
-    y = rows_times(basis)
-    for qq in range(8):
-        for cc in range(2):
-            for k in range(8):
-                row = FB * (8 * cc + k) + 8 * qq
-                s1[cc, qq, k] = y[row : row + 8, :]
+    halves = parts(basis, 2)
+    stacked = jnp.concatenate([halves[0], halves[0], halves[1]], axis=0)
     gram = dot(basis.T, basis)
     for tile in range(NP):
         s1[tile % 2, tile // 2, 8] = gram[8 * tile : 8 * tile + 8, :]
+
+    def half_of_rows(which):
+        y = bdot(an[pl.ds(pl.multiple_of(which * (FH // 2), FH // 2), FH // 2), :], stacked)
+        for qq in range(8):
+            for k in range(8):
+                row = FB * k + 8 * qq
+                s1[which, qq, k] = y[row : row + 8, :]
+
+    half_of_rows(1 - c)
     push(s1.at[1 - c], c1, send.at[5], recv.at[5], other_core)
+    half_of_rows(c)
+    drain(c1, recv.at[5])
+
+    def send_eighths(d):
+        to = wrap(q + d, 8)
+        t1[to] = s1[c, to] + c1[to]
+        push(t1.at[to], r1.at[q], send.at[21], recv.at[21], (group, 2 * to + c))
+
+    each(EIGHTHS, send_eighths)
+    r1[q] = s1[c, q] + c1[q]
     drain(sr, recv.at[3])
     sel_t[...] = ss[...] + sr[...]
     sel[...] = sel_t[...].T
-    drain(c1, recv.at[5])
-    for qq in range(8):
-        t1[qq] = s1[c, qq] + c1[qq]
-
-    def send_eighths(d):
-        to = wrap(q + d, 8)
-        push(t1.at[to], r1.at[q], send.at[21], recv.at[21], (group, 2 * to + c))
-
-    each(EIGHTHS, send_eighths)
-    r1[q] = t1[q]
+    push(sel_t, near.at[0], send.at[15], recv.at[15], (group, wrap(pix + 1, NP)))
+    push(sel_t, near.at[1], send.at[16], recv.at[16], (group, wrap(pix + NP - 1, NP)))
     drain(r1.at[pl.ds(0, 7)], recv.at[21])
     value = r1[0]
     for s in range(1, 8):
@@ -373,6 +414,9 @@
     across = basis.T
     sg[...] = dot(jnp.where(half == 0, across, sel[...]), basis).reshape(NP, 8, RANK)
     to_pix(sg, rg, 11)
+    bs[...] = basis
+    push(bs, near.at[2], send.at[23], recv.at[23], (group, wrap(pix + 1, NP)))
+    push(bs, near.at[3], send.at[24], recv.at[24], (group, wrap(pix + NP - 1, NP)))
     y = rows_times(basis)
     for owner in range(NP):
         for k in range(8):
@@ -393,6 +437,16 @@
     each(RING, send_both)
     k2[...] = total(r2, 12)
     tiles_to_z(k2, zy2, 19)
+
+    def with_near(own, above, below):
+        gap = jnp.zeros((8, 128), F32)
+        rows = [own, above[0:PXH], gap, above[PXH:], below, gap]
+        return jnp.concatenate(rows, axis=0).T
+
+    for k in range(4):
+        drain(near.at[k], recv.at[(15, 16, 23, 24)[k]])
+    selx[...] = with_near(sel_t[...], near[0], near[1])
+    across_x[...] = with_near(bs[...], near[2], near[3])
     drain(ft.at[pl.ds(0, 2 * NP - 1)], recv.at[18])
     start_factor(work, ft[0:NP].reshape(RANK, RANK))
     eliminate(work, linv, 0, 3)
@@ -401,15 +455,14 @@
     eliminate(work, linv, 3, 4)
 
     own = dot_nt(ft[pl.ds(NP + 8 * half, 8)].reshape(FB, RANK), linv[...])
-    ortho_t = dot(linv[...], across)
-    chosen = sel[pl.ds(pl.multiple_of(FB * half, FB), FB), :] - dot(own, ortho_t)
+    ortho_t = dot(linv[...], across_x[...])
+    chosen = selx[pl.ds(pl.multiple_of(FB * half, FB), FB), :] - dot(own, ortho_t)
     shrunk = jnp.where(
         chosen > THRESHOLD,
         chosen - THRESHOLD,
         jnp.where(chosen < -THRESHOLD, chosen + THRESHOLD, 0.0),
     )
     shrunk = shrunk.astype(BF16).astype(F32)
-    shrunk = jnp.concatenate([shrunk, jnp.zeros((FB, 128 - PX), F32)], axis=1)
     for t in range(NZ):
         slab[t] = shrunk[4 * t : 4 * t + 4, :]
 
@@ -426,30 +479,25 @@
     drain(slabs.at[pl.ds(0, NZ - 1)], recv.at[14])
 
     lane = iota((4, 128), 1)
-    strips = []
-    for row in range(2):
+    first, last = pix == 0, pix == NP - 1
+    rows = []
+    for part, start in ((0, 80), (1, 0), (0, 0), (0, 40), (1, 40), (1, 80)):
         tiles = [jnp.zeros((4, 128), F32) for _ in range(5)]
         for t in range(NZ):
             at_tile, shift = (PXH * t) // 128, (PXH * t) % 128
-            piece = slabs[t]
-            turn = (shift - PXH * row) % 128
+            piece = slabs[t, :, 128 * part : 128 * part + 128]
+            turn = (shift - start) % 128
             if turn:
                 piece = pltpu.roll(piece, turn, 1)
             tiles[at_tile] = jnp.where((lane >= shift) & (lane < shift + PXH), piece, tiles[at_tile])
             if shift + PXH > 128:
                 tiles[at_tile + 1] = jnp.where(lane < shift + PXH - 128, piece, tiles[at_tile + 1])
-        strips.append(jnp.concatenate(tiles, axis=1))
-    image[...] = jnp.concatenate(strips, axis=0)
-
-    push(image, halo.at[0], send.at[15], recv.at[15], (group, wrap(pix + 1, NP)))
-    push(image, halo.at[1], send.at[16], recv.at[16], (group, wrap(pix + NP - 1, NP)))
-    drain(halo.at[0], recv.at[15])
-    drain(halo.at[1], recv.at[16])
-    first, last = pix == 0, pix == NP - 1
-    above = jnp.where(first, 0.0, halo[0])
-    below = jnp.where(last, 0.0, halo[1])
-    here = image[...]
-    rows = [above[0:4], above[4:8], here[0:4], here[4:8], below[0:4], below[4:8]]
+        row = jnp.concatenate(tiles, axis=1)
+        if len(rows) < 2:
+            row = jnp.where(first, 0.0, row)
+        if len(rows) > 3:
+            row = jnp.where(last, 0.0, row)
+        rows.append(row)
     place_in_row = iota((4, W), 1)
     for b in range(3):
         for k, row in enumerate(rows):
@@ -485,9 +533,12 @@
             summed = summed + part
         scores_out[:, W * r : W * r + W] = summed
 
-    drain(om.at[pl.ds(0, NZ - 1), 0], send.at[0])
+    @pl.when(carries)
+    def _():
+        drain(om.at[pl.ds(0, NZ - 1), 0], send.at[0])
+
     drain(t_buf.at[pl.ds(0, NZ - 1)], send.at[1])
-    drain(om.at[:, pl.ds(0, 7)], send.at[2])
+    drain(om.at[pl.ds(0, 15)], send.at[2])
     drain(ss, send.at[3])
     drain(xs.at[0], send.at[4])
     drain(c1, send.at[5])
@@ -506,8 +557,8 @@
     drain(zy2.at[pl.ds(0, NZ - 1)], send.at[19])
     drain(fy.at[pl.ds(0, NP - 1)], send.at[20])
     drain(slab.at[pl.ds(0, NZ - 1)], send.at[14])
-    drain(image, send.at[15])
-    drain(image, send.at[16])
+    for sem in (15, 16, 23, 24):
+        drain(bs, send.at[sem])
 
 
 def shards(frames, start_basis, picks, conv_in, bias_in, conv_out, bias_out):
@@ -550,16 +601,18 @@
         vmem((NP, 8, RANK), F32),
         vmem((RANK, 2 * RANK), F32),
         vmem((RANK, RANK), F32),
-        vmem((NZ, 4, 128), F32),
-        vmem((NZ, 4, 128), F32),
-        vmem((8, W), F32),
-        vmem((2, 8, W), F32),
+        vmem((NZ, 4, 256), F32),
+        vmem((NZ, 4, 256), F32),
+        vmem((4, PX, 128), F32),
+        vmem((PX, RANK), F32),
+        vmem((128, 256), F32),
+        vmem((RANK, 256), F32),
         vmem((72, 4 * W), F32),
         vmem((4 * HID, 72), BF16),
         vmem((72, 4 * HID), BF16),
         vmem((4 * HID, 128), F32),
-        pltpu.SemaphoreType.DMA((23,)),
-        pltpu.SemaphoreType.DMA((23,)),
+        pltpu.SemaphoreType.DMA((25,)),
+        pltpu.SemaphoreType.DMA((25,)),
         pltpu.SemaphoreType.DMA((4,)),
         pltpu.SemaphoreType.DMA((8,)),
         pltpu.SemaphoreType.DMA((NZ,)),

time: 108 us -> 105 us (0.972)
  Pallas kernels: 105 us -> 102 us
    pallas_call x1, Pallas kernels: 105 us -> 102 us  [shards(): pl.pallas_call(kernel, out_shape=(jax.ShapeDtypeStruct((FB, RANK), F32),...]
where the time goes in v2:
time: 105 us
  Pallas kernels  102 us (97%)
  local copies, waits for them, and re-layouts  1.99 us (2%)
  between operations  1.3 us (1%)
    pallas_call x1, Pallas kernels, shards(): pl.pallas_call(kernel, out_shape=(jax.ShapeDtypeStruct((FB, RANK), F32),...  102 us

profile of v2, /device:TPU:1, one launch (start us, length us, event | category | flops | bytes accessed | tf_op | source)
XLA Modules:
  0.0 104.8 jit_solution(18353206555471883310)
XLA Ops:
  1.3 101.5 %shard_map.86 = (f32[64,128]{1,0:T(8,128)}, f32[4,1280]{1,0:T(4,128)}) custom-call(f32[64,1280]{1,0:T(8,128)} %frames_hbm.1, f32[64,128]{1,0:T(8,128)} %basis0.1, s32[1,128]{1,0:T(1,128)} %bitcast.6, f32[1,64]{1,0:T(1,128)} %bitcast.7, bf16[9,64]{1,0:T(8,128)(2,1)} %bitcast.5, bf16[9,64]{1,0:T(8,128)(2,1)} %conv_out.1, f32[1,1]{1,0:T(1,128)} %bitcast.4.bias_out), custom_call_target="tpu_custom_call" | custom-call | flops 1500000000 | bytes 1000000 | tf_op jit(solution)/shard_map/pallas_call | solution.py:621
  102.8 0.0 copy-start
  102.8 1.4 %copy.12 = f32[64,128]{1,0:T(8,128)} copy(f32[64,128]{1,0:T(8,128)} %get-tuple-element.4) | data formatting | bytes 65536
  104.2 0.0 copy-done
  104.2 0.6 copy.13
Async XLA Ops:
  102.8 1.4 %copy-start = (f32[4,1280]{1,0:T(4,128)S(1)}, f32[4,1280]{1,0:T(4,128)}, u32[]{:S(2)}) copy-start(f32[4,1280]{1,0:T(4,128)} %get-tuple-element.5) | copy-start | bytes 61444

commit v3 on v2

--- a/solution.py
+++ b/solution.py
@@ -147,10 +147,10 @@
 
 
 def kernel(
-    frames_hbm, basis0, picks_hbm, bias_in_hbm, conv_in, conv_out, bias_out,
+    frames_hbm, basis0, picks_hbm, bias_in_hbm, conv_in_hbm, conv_out_hbm, bias_out_hbm,
     coeffs_out, scores_out,
-    frames, picks, bias_in, t_buf, r_buf, om, at, an, sel_t, sel, xs, xr, ss, sr,
-    s1, c1, t1, r1, k1, zy1, kg1, zg1, yz, yf, gf,
+    frames, picks, bias_in, conv_in, conv_out, bias_out, t_buf, r_buf, om, at, an, sel_t, sel, xs, xr, ss, sr,
+    s1, g1, c1, cg1, t1, r1, k1, zy1, kg1, zg1, yz, yf, gf,
     s2, r2, k2, zy2, sg, rg, kg2, zg2, ft, fy,
     work, linv, slab, slabs, near, bs, selx, across_x, taps, w1, w2, bias_wide,
     send, recv, load, arrive, came,
@@ -164,10 +164,20 @@
     c = pix % 2
     fetch = pltpu.make_async_copy(frames_hbm, frames, load.at[0])
     fetch.start()
-    fetch_picks = pltpu.make_async_copy(picks_hbm, picks, load.at[2])
-    fetch_picks.start()
-    fetch_bias = pltpu.make_async_copy(bias_in_hbm, bias_in, load.at[3])
-    fetch_bias.start()
+    small = [
+        pltpu.make_async_copy(src, dst, load.at[2 + n])
+        for n, (src, dst) in enumerate(
+            (
+                (picks_hbm, picks),
+                (bias_in_hbm, bias_in),
+                (conv_in_hbm, conv_in),
+                (conv_out_hbm, conv_out),
+                (bias_out_hbm, bias_out),
+            )
+        )
+    ]
+    for copy in small:
+        copy.start()
 
     across_group = (1 - half) * NZ + z
     partner = (across_group, pix)
@@ -215,7 +225,7 @@
     def _():
         each(RING, send_basis)
 
-    each(RING[:9], send_frames)
+    each(RING[:4], send_frames)
 
     @pl.when(carries)
     def _():
@@ -225,6 +235,8 @@
 
     r_buf[z] = t_buf[z]
 
+    for copy in small:
+        copy.wait()
     up = (iota((4 * HID, HID), 0) % HID == iota((4 * HID, HID), 1))
     wide = (iota((9, 72), 1) // 8 == iota((9, 72), 0))
     same = iota((4 * HID, 72), 0) // HID == iota((4 * HID, 72), 1) % 8
@@ -239,8 +251,6 @@
     spread = jnp.dot(tall.astype(BF16), conv_out[...], preferred_element_type=F32).astype(BF16)
     spread = jnp.dot(spread, over.astype(BF16), preferred_element_type=F32)
     w2[...] = jnp.where(same, spread, 0.0).astype(BF16)
-    fetch_bias.wait()
-    fetch_picks.wait()
     bias_wide[...] = dot_nt(up.astype(F32), jnp.broadcast_to(bias_in[...], (128, HID)))
     taps[...] = jnp.zeros_like(taps)
 
@@ -261,7 +271,7 @@
 
     for n, d in enumerate(RING):
         spread_basis(d)
-        each(RING[9 + n : 10 + n], send_frames)
+        each(RING[4 + n : 5 + n], send_frames)
 
     low = iota((PXH, 128), 1) < FB
     for k in (4, 3, 5, 2, 6, 1, 7, 0):
@@ -282,8 +292,11 @@
         )
         at[:, pl.ds(pl.multiple_of(128 * m, 128), 128)] = jnp.concatenate(parts(tile, 3), axis=0)
 
-    def frames_times(x):
-        out = bdot(at[...], jnp.concatenate(parts(x, 2), axis=1))
+    def frames_times(x, which=None):
+        picked = at[...]
+        if which is not None:
+            picked = at[:, pl.ds(pl.multiple_of(which * (FH // 2), FH // 2), FH // 2)]
+        out = bdot(picked, jnp.concatenate(parts(x, 2), axis=1))
         out = out[:, 0:RANK] + out[:, RANK:]
         return out[0:PX] + (out[PX : 2 * PX] + out[2 * PX :])
 
@@ -344,9 +357,6 @@
     basis = xs[0] + xr[0]
     halves = parts(basis, 2)
     stacked = jnp.concatenate([halves[0], halves[0], halves[1]], axis=0)
-    gram = dot(basis.T, basis)
-    for tile in range(NP):
-        s1[tile % 2, tile // 2, 8] = gram[8 * tile : 8 * tile + 8, :]
 
     def half_of_rows(which):
         y = bdot(an[pl.ds(pl.multiple_of(which * (FH // 2), FH // 2), FH // 2), :], stacked)
@@ -357,21 +367,28 @@
 
     half_of_rows(1 - c)
     push(s1.at[1 - c], c1, send.at[5], recv.at[5], other_core)
+    gram = dot(basis.T, basis)
+    for tile in range(NP):
+        g1[tile % 2, tile // 2] = gram[8 * tile : 8 * tile + 8, :]
+    push(g1.at[1 - c], cg1, send.at[25], recv.at[25], other_core)
     half_of_rows(c)
     drain(c1, recv.at[5])
+    drain(cg1, recv.at[25])
+
+    def sum_of_cores(to, into):
+        into[to if into is t1 else q, 0:8] = s1[c, to] + c1[to]
+        into[to if into is t1 else q, 8] = g1[c, to] + cg1[to]
 
     def send_eighths(d):
         to = wrap(q + d, 8)
-        t1[to] = s1[c, to] + c1[to]
+        sum_of_cores(to, t1)
         push(t1.at[to], r1.at[q], send.at[21], recv.at[21], (group, 2 * to + c))
 
     each(EIGHTHS, send_eighths)
-    r1[q] = s1[c, q] + c1[q]
+    sum_of_cores(q, r1)
     drain(sr, recv.at[3])
     sel_t[...] = ss[...] + sr[...]
     sel[...] = sel_t[...].T
-    push(sel_t, near.at[0], send.at[15], recv.at[15], (group, wrap(pix + 1, NP)))
-    push(sel_t, near.at[1], send.at[16], recv.at[16], (group, wrap(pix + NP - 1, NP)))
     drain(r1.at[pl.ds(0, 7)], recv.at[21])
     value = r1[0]
     for s in range(1, 8):
@@ -403,11 +420,14 @@
         origin = wrap(q + 8 - d, 8)
         drain(yf.at[ours, origin], arrive.at[d])
         push(yf.at[ours, origin], yf.at[ours, origin], send.at[22], recv.at[22], other_core)
+    mine = frames_times(yf[ours].reshape(FH // 2, RANK), c)
     eliminate(work, linv, 2, 3)
     drain(yf.at[theirs], recv.at[22])
 
-    xs[1] = frames_times(yf[...].reshape(FH, RANK))
+    xs[1] = mine + frames_times(yf[theirs].reshape(FH // 2, RANK), 1 - c)
     push(xs.at[1], xr.at[1], send.at[10], recv.at[10], partner)
+    push(sel_t, near.at[0], send.at[15], recv.at[15], (group, wrap(pix + 1, NP)))
+    push(sel_t, near.at[1], send.at[16], recv.at[16], (group, wrap(pix + NP - 1, NP)))
     eliminate(work, linv, 3, 4)
     drain(xr.at[1], recv.at[10])
     basis = dot_nt(xs[1] + xr[1], linv[...])
@@ -542,6 +562,7 @@
     drain(ss, send.at[3])
     drain(xs.at[0], send.at[4])
     drain(c1, send.at[5])
+    drain(cg1, send.at[25])
     drain(r1.at[pl.ds(0, 7)], send.at[21])
     drain(yf.at[theirs], send.at[22])
     drain(zy1.at[pl.ds(0, NZ - 1)], send.at[6])
@@ -567,6 +588,9 @@
         vmem((FB, 2 * W), F32),
         vmem((1, 128), jnp.int32),
         vmem((1, HID), F32),
+        vmem((9, HID), BF16),
+        vmem((9, HID), BF16),
+        vmem((1, 1), F32),
         vmem((NZ, PXH, 128), F32),
         vmem((NZ, PXH, 128), F32),
         vmem((NZ, 8, 8, RANK), F32),
@@ -578,8 +602,10 @@
         vmem((2, PX, RANK), F32),
         vmem((PX, 128), F32),
         vmem((PX, 128), F32),
-        vmem((2, 8, 9, 8, RANK), F32),
-        vmem((8, 9, 8, RANK), F32),
+        vmem((2, 8, 8, 8, RANK), F32),
+        vmem((2, 8, 8, RANK), F32),
+        vmem((8, 8, 8, RANK), F32),
+        vmem((8, 8, RANK), F32),
         vmem((8, 9, 8, RANK), F32),
         vmem((8, 9, 8, RANK), F32),
         vmem((8, 8, RANK), F32),
@@ -611,9 +637,9 @@
         vmem((4 * HID, 72), BF16),
         vmem((72, 4 * HID), BF16),
         vmem((4 * HID, 128), F32),
-        pltpu.SemaphoreType.DMA((25,)),
-        pltpu.SemaphoreType.DMA((25,)),
-        pltpu.SemaphoreType.DMA((4,)),
+        pltpu.SemaphoreType.DMA((26,)),
+        pltpu.SemaphoreType.DMA((26,)),
+        pltpu.SemaphoreType.DMA((7,)),
         pltpu.SemaphoreType.DMA((8,)),
         pltpu.SemaphoreType.DMA((NZ,)),
     ]
@@ -624,7 +650,7 @@
             jax.ShapeDtypeStruct((FB, RANK), F32),
             jax.ShapeDtypeStruct((4, 2 * W), F32),
         ),
-        in_specs=[pl.BlockSpec(memory_space=pltpu.HBM)] * 4 + [whole] * 3,
+        in_specs=[pl.BlockSpec(memory_space=pltpu.HBM)] * 7,
         out_specs=(whole, whole),
         scratch_shapes=scratch,
         compiler_params=pltpu.CompilerParams(

time: 105 us -> 104 us (level)
  no operation moved by 1% of the time
where the time goes in v3:
time: 104 us
  Pallas kernels  101 us (97%)
  local copies, waits for them, and re-layouts  1.99 us (2%)
  between operations  1.3 us (1%)
    pallas_call x1, Pallas kernels, shards(): pl.pallas_call(kernel, out_shape=(jax.ShapeDtypeStruct((FB, RANK), F32),...  101 us

profile of v3, /device:TPU:1, one launch (start us, length us, event | category | flops | bytes accessed | tf_op | source)
XLA Modules:
  0.0 103.9 jit_solution(9323098315822952210)
XLA Ops:
  1.3 100.6 %shard_map.86 = (f32[64,128]{1,0:T(8,128)}, f32[4,1280]{1,0:T(4,128)}) custom-call(f32[64,1280]{1,0:T(8,128)} %frames_hbm.1, f32[64,128]{1,0:T(8,128)} %basis0.1, s32[1,128]{1,0:T(1,128)} %bitcast.6, f32[1,64]{1,0:T(1,128)} %bitcast.7, bf16[9,64]{1,0:T(8,128)(2,1)} %bitcast.5, bf16[9,64]{1,0:T(8,128)(2,1)} %conv_out_hbm.1, f32[1,1]{1,0:T(1,128)} %bitcast.4.bias_out_hbm), custom_call_target="tpu_custom_call" | custom-call | flops 1500000000 | bytes 1000000 | tf_op jit(solution)/shard_map/pallas_call | solution.py:647
  101.9 0.0 copy-start
  101.9 1.4 %copy.12 = f32[64,128]{1,0:T(8,128)} copy(f32[64,128]{1,0:T(8,128)} %get-tuple-element.4) | data formatting | bytes 65536
  103.3 0.0 copy-done
  103.3 0.6 copy.13
Async XLA Ops:
  101.9 1.4 %copy-start = (f32[4,1280]{1,0:T(4,128)S(1)}, f32[4,1280]{1,0:T(4,128)}, u32[]{:S(2)}) copy-start(f32[4,1280]{1,0:T(4,128)} %get-tuple-element.5) | copy-start | bytes 61444

commit v4 on v3

--- a/solution.py
+++ b/solution.py
@@ -225,7 +225,7 @@
     def _():
         each(RING, send_basis)
 
-    each(RING[:4], send_frames)
+    each(RING[:2], send_frames)
 
     @pl.when(carries)
     def _():
@@ -271,7 +271,7 @@
 
     for n, d in enumerate(RING):
         spread_basis(d)
-        each(RING[4 + n : 5 + n], send_frames)
+        each(RING[2 + n : 3 + n], send_frames)
 
     low = iota((PXH, 128), 1) < FB
     for k in (4, 3, 5, 2, 6, 1, 7, 0):
@@ -450,8 +450,8 @@
 
     def send_both(d):
         to = wrap(pix + d, NP)
+        push(ft.at[place], ft.at[place], send.at[18], recv.at[18], (across_group, to))
         push(ft.at[place], ft.at[place], send.at[18], recv.at[18], (group, to))
-        push(ft.at[place], ft.at[place], send.at[18], recv.at[18], (across_group, to))
 
     push(ft.at[place], ft.at[place], send.at[18], recv.at[18], partner)
     each(RING, send_both)

time: 104 us -> 107 us (1.029)
  Pallas kernels: 101 us -> 103 us
    pallas_call x1, Pallas kernels: 101 us -> 103 us  [shards(): pl.pallas_call(kernel, out_shape=(jax.ShapeDtypeStruct((FB, RANK), F32),...]
where the time goes in v4:
time: 107 us; the launch traced here: 106 us
  Pallas kernels  103 us (96%)
  local copies, waits for them, and re-layouts  1.99 us (2%)
  between operations  1.3 us (1%)
    pallas_call x1, Pallas kernels, shards(): pl.pallas_call(kernel, out_shape=(jax.ShapeDtypeStruct((FB, RANK), F32),...  103 us

profile of v4, /device:TPU:1, one launch (start us, length us, event | category | flops | bytes accessed | tf_op | source)
XLA Modules:
  0.0 106.3 jit_solution(15403271213271565362)
XLA Ops:
  1.3 103.0 %shard_map.86 = (f32[64,128]{1,0:T(8,128)}, f32[4,1280]{1,0:T(4,128)}) custom-call(f32[64,1280]{1,0:T(8,128)} %frames_hbm.1, f32[64,128]{1,0:T(8,128)} %basis0.1, s32[1,128]{1,0:T(1,128)} %bitcast.6, f32[1,64]{1,0:T(1,128)} %bitcast.7, bf16[9,64]{1,0:T(8,128)(2,1)} %bitcast.5, bf16[9,64]{1,0:T(8,128)(2,1)} %conv_out_hbm.1, f32[1,1]{1,0:T(1,128)} %bitcast.4.bias_out_hbm), custom_call_target="tpu_custom_call" | custom-call | flops 1500000000 | bytes 1000000 | tf_op jit(solution)/shard_map/pallas_call | solution.py:647
  104.3 0.0 copy-start
  104.3 1.4 %copy.12 = f32[64,128]{1,0:T(8,128)} copy(f32[64,128]{1,0:T(8,128)} %get-tuple-element.4) | data formatting | bytes 65536
  105.7 0.0 copy-done
  105.7 0.6 copy.13
Async XLA Ops:
  104.3 1.4 %copy-start = (f32[4,1280]{1,0:T(4,128)S(1)}, f32[4,1280]{1,0:T(4,128)}, u32[]{:S(2)}) copy-start(f32[4,1280]{1,0:T(4,128)} %get-tuple-element.5) | copy-start | bytes 61444
